TPU v7x, 32 devices: a whole 2x2x4 slice. The times are simulated.
32 devices in a mesh: req: 4 (over z), vocab: 8 (over y, x, core).
Axes of the slice: x: 2, y: 2, z: 4, core: 2. Of those that a mesh axis runs over, the one named last changes fastest.
Arguments:
- hidden: bfloat16 [16, 384, 2048], P('req', 'vocab'), may hold values from -80 to 80
- norm_gain: float32 [2048], replicated, may hold values from 0.6 to 1.4
- head_weight: bfloat16 [2048, 32000], P(None, 'vocab'), may hold values from -2 to 2
- token_ids: int32 [16, 384], P('req', 'vocab'), may hold values from 0 to 31999
- lengths: int32 [16], replicated, may hold values from 1 to 384, 3840 in all
- group_ids: int32 [16], replicated, may hold values from 0 to 3
Outputs:
- logprob: float32 [16, 384], P('req', 'vocab')
- entropy: float32 [16, 384], P('req', 'vocab')
- centered: float32 [16], replicated
Inputs may be any that keep to these rules, and one draw needn't show every extreme that they name: The lengths sum to 3840; the longest is 384.
All inputs are finite; a program needn't handle non-finite values.
Results may differ from a plain program's by a relative error of at most 0.00093.
Values may be sent and summed in bfloat16 or wider, within the bound.
A program may use at most 128 MiB of HBM per device.

v0:
```python
import jax
import jax.numpy as jnp
from jax import lax
from jax.sharding import PartitionSpec as P

norm_eps = 1e-06


def slice_stats(rows, tokens, weight, offset):
    row_count = rows.shape[0]
    block_len = min(512, row_count)
    columns = jnp.arange(weight.shape[1], dtype=jnp.int32)
    results = []
    for block_start in range(0, row_count, block_len):
        block_rows = rows[block_start : block_start + block_len]
        local_ids = tokens[block_start : block_start + block_len] - offset
        logits = jnp.dot(block_rows, weight, preferred_element_type=jnp.float32)
        row_top = jnp.max(logits, axis=1)
        exps = jnp.exp(logits - row_top[:, None])
        exp_total = jnp.sum(exps, axis=1)
        moment = jnp.sum(exps * logits, axis=1)
        picked = jnp.sum(jnp.where(columns[None, :] == local_ids[:, None], logits, 0.0), axis=1)
        results.append((row_top, exp_total, moment, picked))
    return tuple((jnp.concatenate([item[slot] for item in results]) for slot in range(4)))


def body(hidden, norm_gain, head_weight, token_ids, lengths, group_ids):
    req_dev, pos_dev, model_width = hidden.shape
    vocab_dev = head_weight.shape[1]
    vocab_index = lax.axis_index("vocab")
    req_index = lax.axis_index("req")
    values = hidden.astype(jnp.float32)
    squares = jnp.mean(values * values, axis=-1, keepdims=True)
    normed = (values * lax.rsqrt(squares + norm_eps) * norm_gain).astype(jnp.bfloat16)
    own_rows = req_dev * pos_dev
    flat_rows = normed.reshape(own_rows, model_width)
    flat_tokens = token_ids.reshape(own_rows)
    offset = vocab_index * vocab_dev
    fresh = slice_stats(
        lax.all_gather(flat_rows, "vocab", axis=0, tiled=True),
        lax.all_gather(flat_tokens, "vocab", axis=0, tiled=True),
        head_weight,
        offset,
    )
    maxima, sums, moments, picked = tuple((new_part for new_part in fresh))
    own_start = vocab_index * own_rows
    row_top = lax.pmax(maxima, "vocab")
    rescale = jnp.exp(maxima - row_top)
    exp_total, moment, token_logit = lax.psum((sums * rescale, moments * rescale, picked), "vocab")
    row_top = lax.dynamic_slice_in_dim(row_top, own_start, own_rows)
    exp_total = lax.dynamic_slice_in_dim(exp_total, own_start, own_rows)
    moment = lax.dynamic_slice_in_dim(moment, own_start, own_rows)
    token_logit = lax.dynamic_slice_in_dim(token_logit, own_start, own_rows)
    log_total = row_top + jnp.log(exp_total)
    raw_logprob = (token_logit - log_total).reshape(req_dev, pos_dev)
    raw_entropy = (log_total - moment / exp_total).reshape(req_dev, pos_dev)
    positions = vocab_index * pos_dev + jnp.arange(pos_dev, dtype=jnp.int32)
    own_lengths = lax.dynamic_slice_in_dim(lengths, req_index * req_dev, req_dev)
    is_live = positions[None, :] < own_lengths[:, None]
    logprob = jnp.where(is_live, raw_logprob, 0.0)
    entropy = jnp.where(is_live, raw_entropy, 0.0)
    partial_sums = jnp.sum(logprob, axis=1)
    request_count = lengths.shape[0]
    global_rows = req_index * req_dev + jnp.arange(req_dev, dtype=jnp.int32)
    slots = jnp.arange(request_count, dtype=jnp.int32)
    placed = jnp.sum(
        jnp.where(slots[None, :] == global_rows[:, None], partial_sums[:, None], 0.0), axis=0
    )
    seq_sum = lax.psum(placed, ("req", "vocab"))
    same = (group_ids[:, None] == group_ids[None, :]).astype(jnp.float32)
    members = jnp.sum(same, axis=1)
    group_mean = jnp.sum(same * seq_sum[None, :], axis=1) / members
    spread = jnp.sum(same * (seq_sum[None, :] - group_mean[:, None]) ** 2, axis=1) / members
    group_std = jnp.maximum(jnp.sqrt(spread), 1.0)
    centered = (seq_sum - group_mean) / group_std
    return (logprob, entropy, centered)


def solution(mesh):
    return jax.shard_map(
        body,
        mesh=mesh,
        in_specs=(P("req", "vocab", None), P(), P(None, "vocab"), P("req", "vocab"), P(), P()),
        out_specs=(P("req", "vocab"), P("req", "vocab"), P()),
        check_vma=False,
    )
```

profile of v0, /device:TPU:0, one launch (start us, length us, event | category | flops | bytes accessed | tf_op | source)
XLA Modules:
  0.0 199.9 jit_solution(13699862402432941046)
XLA Ops:
  7.2 1.4 fusion.9
  8.6 2.3 %fusion.11 = bf16[4,48,2048]{2,1,0:T(8,128)(2,1)} fusion(bf16[4,48,2048]{2,1,0:T(8,128)(2,1)} %param.6, f32[2048]{0:T(1024)} %param.7, f32[4,48]{1,0:T(4,128)S(1)} %add_rsqrt_fusion), kind=kLoop, calls=%fused_computation.25 | loop fusion | flops 1572864 | bytes 1581824 | tf_op jit(solution)/shard_map/convert_element_type | solution.py:34
  10.9 0.8 reshape.55
  11.7 1.2 dynamic-slice
  13.5 0.7 dynamic_slice.15
  14.3 0.2 dynamic-update-slice
  14.5 9.6 %all-reduce = s32[1536]{0:T(1024)S(1)} all-reduce(s32[1536]{0:T(1024)S(1)} %dynamic-update-slice), channel_id=1, replica_groups=mesh['req'=4,'vocab'=8] {'vocab'}, use_global_device_ids=true, to_apply=%add | all-reduce | flops 1536 | bytes 12288
  24.1 35.2 %all-gather.2.cloned.1.call-done = bf16[1536,2048]{1,0:T(8,128)(2,1)} async-done(((bf16[192,2048]{1,0:T(8,128)(2,1)}), bf16[1536,2048]{1,0:T(8,128)(2,1)}) %all-gather.2.cloned.1.call-update) | async-done | bytes 6291472 | tf_op jit(solution)/shard_map/all_gather | solution.py:40
  59.3 15.9 %fusion.16 = (f32[512]{0:T(512)S(1)}, f32[512,4000]{0,1:T(8,128)}) fusion(bf16[2048,4000]{0,1:T(8,128)(2,1)} %param.8, bf16[1536,2048]{1,0:T(8,128)(2,1)} %all-gather.2.cloned.1.call-done), kind=kOutput, calls=%fused_computation.52 | convolution fusion | flops 8390655488 | bytes 26675200 | tf_op jit(solution)/shard_map/dot_general | solution.py:17
  75.2 14.9 %fusion.17 = (f32[512]{0:T(512)S(1)}, f32[512,4000]{0,1:T(8,128)}) fusion(bf16[2048,4000]{0,1:T(8,128)(2,1)} %param.8, bf16[1536,2048]{1,0:T(8,128)(2,1)} %all-gather.2.cloned.1.call-done), kind=kOutput, calls=%fused_computation.53 | convolution fusion | flops 8390655488 | bytes 26675200 | tf_op jit(solution)/shard_map/dot_general | solution.py:17
  90.1 12.9 %fusion.18 = (f32[512]{0:T(512)S(1)}, f32[512,4000]{0,1:T(8,128)}) fusion(bf16[2048,4000]{0,1:T(8,128)(2,1)S(1)} %bitcast.7, bf16[1536,2048]{1,0:T(8,128)(2,1)} %all-gather.2.cloned.1.call-done), kind=kOutput, calls=%fused_computation.54 | convolution fusion | flops 8390655488 | bytes 26675200 | tf_op jit(solution)/shard_map/dot_general | solution.py:17
  103.0 13.4 %pmax.7 = f32[1536]{0:T(1024)S(1)} all-reduce(f32[1536]{0:T(1024)S(1)} %pad_maximum_fusion.1), channel_id=1, replica_groups=mesh['req'=4,'vocab'=8] {'vocab'}, use_global_device_ids=true, to_apply=%region_8.9 | all-reduce | flops 1536 | bytes 12288 | tf_op jit(solution)/shard_map/pmax | solution.py:47
  116.4 5.0 %multiply_reduce_fusion.2 = (f32[512]{0:T(512)S(1)}, f32[512]{0:T(512)S(1)}, f32[512]{0:T(512)S(1)}) fusion(f32[512,4000]{0,1:T(8,128)} %get-tuple-element.32, f32[512]{0:T(512)S(1)} %get-tuple-element.31, s32[512]{0:T(512)S(1)} %get-tuple-element.23), kind=kLoop, calls=%fused_computation.2 | loop fusion | flops 14334464 | bytes 8202240 | tf_op jit(solution)/shard_map/reduce_sum | solution.py:21
  121.4 0.7 copy-done
  122.1 7.1 %multiply_reduce_fusion = (f32[512]{0:T(512)S(1)}, f32[512]{0:T(512)S(1)}, f32[512]{0:T(512)S(1)}, f32[512]{0:T(512)S(1)}, f32[512]{0:T(512)S(1)}, /*index=5*/f32[512]{0:T(512)S(1)}) fusion(f32[512,4000]{0,1:T(8,128)S(1)} %copy-done, f32[512]{0:T(512)S(1)} %get-tuple-element.27, s32[512]{0:T(512)S(1)} %get-tuple-element.25, f32[512,4000]{0,1:T(8,128)} %get-tuple-element.30, ...), kind=kLoop, calls=%fused_computation | loop fusion | flops 28668928 | bytes 16404480 | tf_op jit(solution)/shard_map/reduce_sum | solution.py:21
  129.3 22.4 %all-reduce.1 = (f32[1536]{0:T(1024)S(1)}, f32[1536]{0:T(1024)S(1)}, f32[1536]{0:T(1024)S(1)}) all-reduce(f32[1536]{0:T(1024)S(1)} %pad_maximum_fusion, f32[1536]{0:T(1024)S(1)} %get-tuple-element.22, f32[1536]{0:T(1024)S(1)} %get-tuple-element.21), channel_id=1, replica_groups=mesh['req'=4,'vocab'=8] {'vocab'}, use_global_device_ids=true, to_apply=%region_4.5 | all-reduce | flops 4608 | bytes 36864 | tf_op jit(solution)/shard_map/psum | solution.py:49
  151.8 0.1 reshape.53
  151.9 0.1 reshape.54
  152.0 0.8 fusion.15
  152.7 0.1 select_reduce_fusion.3
  152.8 39.3 %psum.31 = f32[16]{0:T(128)S(1)} all-reduce(f32[16]{0:T(128)S(1)} %select_reduce_fusion.3), channel_id=1, replica_groups=mesh['req'=4,'vocab'=8] {'req','vocab'}, use_global_device_ids=true, to_apply=%region_19.20 | all-reduce | flops 16 | bytes 128 | tf_op jit(solution)/shard_map/psum | solution.py:69
  192.1 0.2 fusion.13
  192.3 0.2 fusion.14
  192.5 0.5 maximum_divide_fusion
  (24 shorter events, 0.2 us)
Async XLA Ops:
  7.2 52.1 %all-gather.2.cloned.1.call-start = ((), (), s32[]{:S(2)}) async-start(), calls=%async_computation | async-start | bytes 7077888 | tf_op jit(solution)/shard_map/all_gather | solution.py:40
  59.3 30.9 %slice-start = ((s8[16384000]{0:T(1024)(128)(4,1)}), s8[4194304]{0:T(1024)(128)(4,1)S(1)}, s32[]{:S(2)}) async-start(s8[16384000]{0:T(1024)(128)(4,1)} %bitcast.6), calls=%async_computation.1 | async-start | bytes 8388608
  59.3 30.9 %slice-start.1 = ((s8[16384000]{0:T(1024)(128)(4,1)}), s8[4194304]{0:T(1024)(128)(4,1)S(1)}, s32[]{:S(2)}) async-start(s8[16384000]{0:T(1024)(128)(4,1)} %bitcast.6), calls=%async_computation.2 | async-start | bytes 8388608
  59.3 30.9 %slice-start.2 = ((s8[16384000]{0:T(1024)(128)(4,1)}), s8[4194304]{0:T(1024)(128)(4,1)S(1)}, s32[]{:S(2)}) async-start(s8[16384000]{0:T(1024)(128)(4,1)} %bitcast.6), calls=%async_computation.3 | async-start | bytes 8388608
  75.2 15.0 %slice-start.3 = ((s8[16384000]{0:T(1024)(128)(4,1)}), s8[3801088]{0:T(1024)(128)(4,1)S(1)}, s32[]{:S(2)}) async-start(s8[16384000]{0:T(1024)(128)(4,1)} %bitcast.6), calls=%async_computation.4 | async-start | bytes 7602176
  116.4 5.7 %copy-start = (f32[512,4000]{0,1:T(8,128)S(1)}, f32[512,4000]{0,1:T(8,128)}, u32[]{:S(2)}) copy-start(f32[512,4000]{0,1:T(8,128)} %get-tuple-element.28) | copy-start | bytes 24576004
  122.1 70.0 %copy-start.1 = (s32[16]{0:T(128)S(1)}, s32[16]{0:T(128)}, u32[]{:S(2)}) copy-start(s32[16]{0:T(128)} %param.11) | copy-start | bytes 196
Sparse Core Ops, SparseCore 0:
  11.0 48.2 all-gather.1
where the time goes:
time: 200 us
  blocking collectives  84.6 us (42%)
  matrix products  43.7 us (22%)
  waiting for transfers between devices  35.2 us (18%)
  other arithmetic  17.7 us (9%)
  between operations  14.8 us (7%)
  local copies, waits for them, and re-layouts  3.82 us (2%)
    dot_general x3, matrix products, slice_stats(): logits = jnp.dot(block_rows, weight, preferred_element_type=jnp.float32)  43.7 us
    psum x1, blocking collectives, body(): seq_sum = lax.psum(placed, ('req', 'vocab'))  39.3 us
    all_gather x1, waiting for transfers between devices, body(): lax.all_gather(flat_rows, 'vocab', axis=0, tiled=True)  35.2 us
    psum x1, blocking collectives, body(): lax.psum((sums * rescale, moments * rescale, picked), 'vocab')  22.4 us
    pmax x1, blocking collectives, body(): row_top = lax.pmax(maxima, 'vocab')  13.4 us
    reduce_sum x2, other arithmetic, slice_stats(): moment = jnp.sum(exps * logits, axis=1)  12.1 us
    unnamed x1, blocking collectives  9.57 us
  transfers between devices with their start and end apart: 1, of which 1 were waited for; matrix products, arithmetic and copies ran while one was open for 1% of the time, Pallas kernels for 0%

commit v1 on v0

--- a/solution.py
+++ b/solution.py
@@ -1,9 +1,389 @@
+import functools
 import jax
 import jax.numpy as jnp
 from jax import lax
 from jax.sharding import PartitionSpec as P
+from jax.experimental import pallas as pl
+from jax.experimental.pallas import tpu as pltpu
 
 norm_eps = 1e-06
+BLOCK = 192
+MESH_ID = pl.DeviceIdType.MESH
+LOW = -1e30
+LANES = 128
+CHUNK = 512
+STRIP = 32
+QUARTERS = 4
+
+
+def piece_order():
+    order = [(0, q) for q in range(4)] + [(1, q) for q in range(4)]
+    for k in range(4):
+        other = (k + 2) % 4
+        order += [(2, k), (4, other), (3, k), (5, other)]
+    for k in range(2):
+        order += [(6, k), (6, k + 2), (7, k), (7, k + 2)]
+    return order
+
+
+def fused_kernel(
+    planes, lengths_ref, groups_ref, hidden_ref, gain_ref, tokens_ref, weight_ref,
+    logprob_ref, entropy_ref, centered_ref,
+    rows, weight, logits_a, logits_b, top_lane, top_row, sum_acc, mom_acc, pick_acc, ids,
+    tokens, stat_out, stat_in, part, plane_sums,
+    weight_sem, row_send, row_recv, token_send, token_recv, stat_send, stat_recv,
+    part_send, part_recv, plane_send, plane_recv,
+):
+    req_dev, pos_dev, width = hidden_ref.shape
+    vocab_dev = weight_ref.shape[1]
+    block = ids.shape[0]
+    per_block = block // pos_dev
+    plane = lax.axis_index("req")
+    me = lax.axis_index("vocab")
+    order = piece_order()
+    slot = {piece: i * pos_dev for i, piece in enumerate(order)}
+    blocks = len(order) // per_block
+    full = vocab_dev // CHUNK
+    tail_start = full * CHUNK
+
+    yy, xx, cc = me // 4, (me // 2) % 2, me % 2
+
+    def partner(rel):
+        y = 1 - yy if rel & 4 else yy
+        x = 1 - xx if rel & 2 else xx
+        c = 1 - cc if rel & 1 else cc
+        return (plane, y * 4 + x * 2 + c)
+
+    bounds = list(range(0, tail_start, 2 * CHUNK)) + [vocab_dev]
+    if len(bounds) > 2 and bounds[-1] - bounds[-2] < 128:
+        bounds.pop(-2)
+    spans = list(zip(bounds[:-1], bounds[1:]))
+    weight_copies = [
+        pltpu.make_async_copy(
+            weight_ref.at[:, lo:hi], weight.at[:, lo:hi], weight_sem.at[i]
+        )
+        for i, (lo, hi) in enumerate(spans)
+    ]
+    for copy in weight_copies:
+        copy.start()
+
+    barrier = pltpu.get_barrier_semaphore()
+    for rel in range(1, 8):
+        pl.semaphore_signal(barrier, inc=1, device_id=partner(rel), device_id_type=MESH_ID)
+    for step in range(1, planes):
+        pl.semaphore_signal(
+            barrier, inc=1, device_id=(lax.rem(plane + step, planes), me), device_id_type=MESH_ID
+        )
+
+    def normalize(q):
+        values = hidden_ref[q].astype(jnp.float32)
+        squares = jnp.mean(values * values, axis=1, keepdims=True)
+        normed = values * lax.rsqrt(squares + norm_eps) * gain_ref[...]
+        rows[slot[(0, q)] : slot[(0, q)] + pos_dev, :] = normed.astype(jnp.bfloat16)
+
+    started = []
+    send_count = [0]
+
+    def send_piece(piece, rel, landing):
+        index = send_count[0]
+        send_count[0] += 1
+        copy = pltpu.make_async_remote_copy(
+            src_ref=rows.at[pl.ds(slot[piece], pos_dev), :],
+            dst_ref=rows.at[pl.ds(slot[landing], pos_dev), :],
+            send_sem=row_send.at[index],
+            recv_sem=row_recv.at[order.index(landing)],
+            device_id=partner(rel),
+            device_id_type=MESH_ID,
+        )
+        copy.start()
+        started.append(copy)
+
+    def await_piece(piece):
+        view = rows.at[pl.ds(slot[piece], pos_dev), :]
+        pltpu.make_async_copy(view, view, row_recv.at[order.index(piece)]).wait()
+
+    normalize(0)
+    normalize(2)
+    tokens[0, :, :] = jnp.zeros(tokens.shape[1:], jnp.int32)
+    tokens[0, 0:req_dev, 0:pos_dev] = tokens_ref[...]
+    pl.semaphore_wait(barrier, 7 + planes - 1)
+    for q_x, q_y in ((0, 2), (1, 3), (2, 0), (3, 1)):
+        if q_x == 1:
+            normalize(1)
+            normalize(3)
+        send_piece((0, q_x), 2, (2, q_x))
+        send_piece((0, q_y), 4, (4, q_y))
+        if q_x == 0:
+            for rel in range(1, 8):
+                copy = pltpu.make_async_remote_copy(
+                    src_ref=tokens.at[0], dst_ref=tokens.at[rel],
+                    send_sem=token_send.at[rel], recv_sem=token_recv.at[rel],
+                    device_id=partner(rel), device_id_type=MESH_ID,
+                )
+                copy.start()
+                started.append(copy)
+        send_piece((0, q_x), 1, (1, q_x))
+
+    def forward(index):
+        for rel, q in order[index * 4 : index * 4 + 4]:
+            if rel % 2:
+                continue
+            await_piece((rel, q))
+            if rel == 2 and q < 2:
+                send_piece((rel, q), 4, (6, q))
+            if rel == 4 and q >= 2:
+                send_piece((rel, q), 2, (6, q))
+            send_piece((rel, q), 1, (rel + 1, q))
+
+    lane_row = lax.broadcasted_iota(jnp.int32, (pos_dev, LANES), 1)
+    eye = lane_row == lax.broadcasted_iota(jnp.int32, (pos_dev, LANES), 0)
+    logits_a[:, full * CHUNK :] = jnp.full((block, logits_a.shape[1] - full * CHUNK), LOW, jnp.float32)
+    logits_b[:, full * CHUNK :] = jnp.full((block, logits_b.shape[1] - full * CHUNK), LOW, jnp.float32)
+    for rel in range(8):
+        stat_out[rel, :, :] = jnp.zeros(stat_out.shape[1:], jnp.float32)
+
+    def matmul_part(index, out, start, size):
+        acc = jnp.dot(
+            rows[index * block : (index + 1) * block, :],
+            weight[:, pl.ds(start, size)],
+            preferred_element_type=jnp.float32,
+        )
+        out[:, pl.ds(start, size)] = acc
+        whole = size // LANES * LANES
+        if whole:
+            top = acc[:, 0:LANES]
+            for j in range(LANES, whole, LANES):
+                top = jnp.maximum(top, acc[:, j : j + LANES])
+            top_lane[...] = jnp.maximum(top_lane[...], top)
+        if whole != size:
+            top_lane[...] = jnp.maximum(top_lane[...], out[:, pl.ds(start + whole, LANES)])
+
+    def stats_part(source, start):
+        for strip in range(0, block, STRIP):
+            r = slice(strip, strip + STRIP)
+            total, moment, picked = sum_acc[r, :], mom_acc[r, :], pick_acc[r, :]
+            top, local = top_row[r, :], ids[r, :]
+            for j in range(0, CHUNK, LANES):
+                value = source[r, pl.ds(start + j, LANES)]
+                shifted = value - top
+                grown = jnp.exp(shifted)
+                total = total + grown
+                moment = moment + grown * shifted
+                picked = jnp.where(local == start + j, value, picked)
+            sum_acc[r, :], mom_acc[r, :], pick_acc[r, :] = total, moment, picked
+
+    def begin_stats(index):
+        top = jnp.max(top_lane[...], axis=1, keepdims=True)
+        top_row[...] = jnp.broadcast_to(top, top_row.shape)
+        zero = jnp.zeros((block, LANES), jnp.float32)
+        sum_acc[...] = zero
+        mom_acc[...] = zero
+        pick_acc[...] = zero
+        for i in range(per_block):
+            rel, q = order[index * per_block + i]
+            line = tokens[rel, q : q + 1, :].astype(jnp.float32)
+            column = jnp.sum(jnp.where(eye, line, 0.0), axis=1, keepdims=True).astype(jnp.int32)
+            local = column - me * vocab_dev
+            local = jnp.where(local < vocab_dev, local, -1)
+            ids[i * pos_dev : (i + 1) * pos_dev, :] = local - lane_row
+
+    def end_stats(index):
+        for i in range(per_block):
+            rel, q = order[index * per_block + i]
+            r = slice(i * pos_dev, (i + 1) * pos_dev)
+            columns = (
+                top_row[r, :],
+                jnp.sum(sum_acc[r, :], axis=1, keepdims=True),
+                jnp.sum(mom_acc[r, :], axis=1, keepdims=True),
+                jnp.sum(pick_acc[r, :], axis=1, keepdims=True),
+            )
+            for s, column in enumerate(columns):
+                line = jnp.sum(jnp.where(eye, column, 0.0), axis=0, keepdims=True)
+                stat_out[rel, s * 8 + q : s * 8 + q + 1, :] = line
+        done = order[: (index + 1) * per_block]
+        for rel in range(1, 8):
+            last = max(order.index((rel, q)) for q in range(4)) // per_block
+            if last == index:
+                copy = pltpu.make_async_remote_copy(
+                    src_ref=stat_out.at[rel], dst_ref=stat_in.at[rel],
+                    send_sem=stat_send.at[rel], recv_sem=stat_recv.at[rel],
+                    device_id=partner(rel), device_id_type=MESH_ID,
+                )
+                copy.start()
+                started.append(copy)
+
+    padded = logits_a.shape[1] // CHUNK
+    for index in range(blocks + 1):
+        current, previous = (logits_a, logits_b) if index % 2 == 0 else (logits_b, logits_a)
+        if 1 <= index < blocks:
+            ahead = range((index + 1) * per_block // 4, (index + 2) * per_block // 4)
+            for part_index in ahead:
+                if 2 <= part_index < len(order) // 4:
+                    forward(part_index)
+            for piece in order[index * per_block : (index + 1) * per_block]:
+                if piece[0] % 2:
+                    await_piece(piece)
+        if index == 1:
+            for rel in range(1, 8):
+                pltpu.make_async_copy(tokens.at[rel], tokens.at[rel], token_recv.at[rel]).wait()
+        if index > 0:
+            begin_stats(index - 1)
+        if index == blocks:
+            @pl.loop(0, padded)
+            def drain(n):
+                stats_part(previous, pl.multiple_of(n * CHUNK, CHUNK))
+        else:
+            top_lane[...] = jnp.full((block, LANES), LOW, jnp.float32)
+            if index == 0:
+                for copy, (lo, hi) in zip(weight_copies, spans):
+                    copy.wait()
+                    stop = min(hi, tail_start)
+
+                    @pl.loop(lo // CHUNK, stop // CHUNK)
+                    def first(n):
+                        matmul_part(0, current, pl.multiple_of(n * CHUNK, CHUNK), CHUNK)
+            else:
+                @pl.loop(0, full)
+                def steady(n):
+                    start = pl.multiple_of(n * CHUNK, CHUNK)
+                    matmul_part(index, current, start, CHUNK)
+                    stats_part(previous, start)
+            if tail_start < vocab_dev:
+                matmul_part(index, current, tail_start, vocab_dev - tail_start)
+            if index > 0:
+                for n in range(full, padded):
+                    stats_part(previous, n * CHUNK)
+        if index > 0:
+            end_stats(index - 1)
+
+    for rel in range(1, 8):
+        pltpu.make_async_copy(stat_in.at[rel], stat_in.at[rel], stat_recv.at[rel]).wait()
+
+    def held(rel, s):
+        source = stat_out if rel == 0 else stat_in
+        return source[rel, s * 8 : s * 8 + 8, :]
+
+    top = held(0, 0)
+    for rel in range(1, 8):
+        top = jnp.maximum(top, held(rel, 0))
+    total = moment = picked = None
+    for rel in range(8):
+        gap = held(rel, 0) - top
+        scale = jnp.exp(gap)
+        one = held(rel, 1) * scale
+        two = held(rel, 2) * scale + one * gap
+        three = held(rel, 3)
+        total = one if total is None else total + one
+        moment = two if moment is None else moment + two
+        picked = three if picked is None else picked + three
+    row_id = lax.broadcasted_iota(jnp.int32, (8, LANES), 0)
+    lane_id = lax.broadcasted_iota(jnp.int32, (8, LANES), 1)
+    limit = jnp.zeros((8, LANES), jnp.int32)
+    for j in range(req_dev):
+        limit = jnp.where(row_id == j, lengths_ref[plane * req_dev + j], limit)
+    live = (lane_id < pos_dev) & (lane_id + me * pos_dev < limit)
+    total = jnp.where(live, total, 1.0)
+    log_sum = jnp.log(total)
+    logprob = jnp.where(live, picked - top - log_sum, 0.0)
+    entropy = jnp.where(live, log_sum - moment / total, 0.0)
+    logprob_ref[...] = logprob[0:req_dev, 0:pos_dev]
+    entropy_ref[...] = entropy[0:req_dev, 0:pos_dev]
+
+    part[0, :, :] = jnp.broadcast_to(jnp.sum(logprob, axis=1, keepdims=True), (8, LANES))
+    for rel in range(1, 8):
+        copy = pltpu.make_async_remote_copy(
+            src_ref=part.at[0], dst_ref=part.at[rel],
+            send_sem=part_send.at[rel], recv_sem=part_recv.at[rel],
+            device_id=partner(rel), device_id_type=MESH_ID,
+        )
+        copy.start()
+        started.append(copy)
+    for rel in range(1, 8):
+        pltpu.make_async_copy(part.at[rel], part.at[rel], part_recv.at[rel]).wait()
+    pairs = [part[2 * i] + part[2 * i + 1] for i in range(4)]
+    plane_sums[0, :, :] = (pairs[0] + pairs[1]) + (pairs[2] + pairs[3])
+    for step in range(1, planes):
+        copy = pltpu.make_async_remote_copy(
+            src_ref=plane_sums.at[0], dst_ref=plane_sums.at[step],
+            send_sem=plane_send.at[step], recv_sem=plane_recv.at[step],
+            device_id=(lax.rem(plane + step, planes), me), device_id_type=MESH_ID,
+        )
+        copy.start()
+        started.append(copy)
+    for step in range(1, planes):
+        pltpu.make_async_copy(plane_sums.at[step], plane_sums.at[step], plane_recv.at[step]).wait()
+
+    count = planes * req_dev
+    pieces = []
+    for z in range(planes):
+        chosen = plane_sums[0]
+        for step in range(1, planes):
+            chosen = jnp.where(lax.rem(z + step, planes) == plane, plane_sums[step], chosen)
+        pieces.append(chosen[0:req_dev, :])
+    column = jnp.concatenate(pieces, axis=0)
+    row16 = lax.broadcasted_iota(jnp.int32, (count, LANES), 0)
+    lane16 = lax.broadcasted_iota(jnp.int32, (count, LANES), 1)
+    across = jnp.sum(jnp.where(row16 == lane16, column, 0.0), axis=0, keepdims=True)
+    group_column = jnp.full((count, LANES), -1, jnp.int32)
+    group_row = jnp.full((count, LANES), -2, jnp.int32)
+    for j in range(count):
+        group_column = jnp.where(row16 == j, groups_ref[j], group_column)
+        group_row = jnp.where(lane16 == j, groups_ref[j], group_row)
+    same = (group_column == group_row).astype(jnp.float32)
+    members = jnp.sum(same, axis=0, keepdims=True)
+    members = jnp.maximum(members, 1.0)
+    mean = jnp.sum(same * column, axis=0, keepdims=True) / members
+    spread = jnp.sum(same * (column - mean) ** 2, axis=0, keepdims=True) / members
+    centered = (across - mean) / jnp.maximum(jnp.sqrt(spread), 1.0)
+    centered_ref[...] = centered[:, 0:count]
+    for copy in started:
+        copy.wait_send()
+
+
+def fused_body(planes, block, hidden, norm_gain, head_weight, token_ids, lengths, group_ids):
+    req_dev, pos_dev, width = hidden.shape
+    vocab_dev = head_weight.shape[1]
+    padded = -(-vocab_dev // CHUNK) * CHUNK
+    smem = pl.BlockSpec(memory_space=pltpu.SMEM)
+    vmem = pl.BlockSpec(memory_space=pltpu.VMEM)
+    dma = pltpu.SemaphoreType.DMA
+    wide = pltpu.VMEM((block, LANES), jnp.float32)
+    gathered = 8 * req_dev * pos_dev
+    logprob, entropy, centered = pl.pallas_call(
+        functools.partial(fused_kernel, planes),
+        out_shape=(
+            jax.ShapeDtypeStruct((req_dev, pos_dev), jnp.float32),
+            jax.ShapeDtypeStruct((req_dev, pos_dev), jnp.float32),
+            jax.ShapeDtypeStruct((1, planes * req_dev), jnp.float32),
+        ),
+        in_specs=[smem, smem, vmem, vmem, vmem, pl.BlockSpec(memory_space=pl.ANY)],
+        out_specs=(vmem, vmem, vmem),
+        scratch_shapes=[
+            pltpu.VMEM((gathered, width), jnp.bfloat16),
+            pltpu.VMEM((width, vocab_dev), jnp.bfloat16),
+            pltpu.VMEM((block, padded), jnp.float32),
+            pltpu.VMEM((block, padded), jnp.float32),
+            wide, wide, wide, wide, wide,
+            pltpu.VMEM((block, LANES), jnp.int32),
+            pltpu.VMEM((8, 8, LANES), jnp.int32),
+            pltpu.VMEM((8, 32, LANES), jnp.float32),
+            pltpu.VMEM((8, 32, LANES), jnp.float32),
+            pltpu.VMEM((8, 8, LANES), jnp.float32),
+            pltpu.VMEM((planes, 8, LANES), jnp.float32),
+            dma((8,)), dma((32,)), dma((32,)), dma((8,)), dma((8,)), dma((8,)), dma((8,)),
+            dma((8,)), dma((8,)), dma((planes,)), dma((planes,)),
+        ],
+        compiler_params=pltpu.CompilerParams(
+            collective_id=0, has_side_effects=True, vmem_limit_bytes=56 * 1024 * 1024
+        ),
+        cost_estimate=pl.CostEstimate(
+            flops=2 * gathered * width * vocab_dev,
+            bytes_accessed=2 * width * vocab_dev,
+            transcendentals=gathered * vocab_dev,
+        ),
+        name="fused_scores",
+    )(lengths, group_ids, hidden, norm_gain.reshape(1, width), token_ids, head_weight)
+    return logprob, entropy, centered.reshape(planes * req_dev)
 
 
 def slice_stats(rows, tokens, weight, offset):
@@ -77,8 +457,11 @@
 
 
 def solution(mesh):
+    plan = body
+    if mesh.shape["vocab"] == 8:
+        plan = functools.partial(fused_body, mesh.shape["req"], BLOCK)
     return jax.shard_map(
-        body,
+        plan,
         mesh=mesh,
         in_specs=(P("req", "vocab", None), P(), P(None, "vocab"), P("req", "vocab"), P(), P()),
         out_specs=(P("req", "vocab"), P("req", "vocab"), P()),

time: 200 us -> 89.4 us (0.45)
  blocking collectives: 84.6 us -> 0 us
  Pallas kernels: 0 us -> 63.1 us
  matrix products: 43.7 us -> 0 us
  waiting for transfers between devices: 35.2 us -> 0 us
  local copies, waits for them, and re-layouts: 3.82 us -> 25 us
  other arithmetic: 17.7 us -> 0 us
  between operations: 14.8 us -> 0.64 us
    pallas_call x0 -> x1, Pallas kernels: none -> 63.1 us  [fused_body(): pl.pallas_call(functools.partial(fused_kernel, planes), out_shape=(jax.Sh...]
    psum x2 -> x0, blocking collectives: 61.7 us -> none  [the longest x1 39.3 us: body(): seq_sum = lax.psum(placed, ('req', 'vocab'))]
    dot_general x3 -> x0, matrix products: 43.7 us -> none  [slice_stats(): logits = jnp.dot(block_rows, weight, preferred_element_type=jnp.float32)]
    all_gather x1 -> x0, waiting for transfers between devices: 35.2 us -> none  [body(): lax.all_gather(flat_rows, 'vocab', axis=0, tiled=True)]
    unnamed x15 -> x4, local copies, waits for them, and re-layouts: 2.16 us -> 25 us
    reduce_sum x7 -> x0, other arithmetic: 14.7 us -> none  [the longest x2 12.1 us: slice_stats(): moment = jnp.sum(exps * logits, axis=1)]
    pmax x1 -> x0, blocking collectives: 13.4 us -> none  [body(): row_top = lax.pmax(maxima, 'vocab')]
    unnamed x1 -> x0, blocking collectives: 9.57 us -> none
  transfers between devices with their start and end apart: 1 -> 0, of which waited for: 1 -> 0; matrix products, arithmetic and copies ran while one was open for 1% -> 0% of each run, Pallas kernels for 0% -> 0%
where the time goes in v1:
time: 89.4 us; the launch traced here: 88.7 us
  Pallas kernels  63.1 us (71%)
  local copies, waits for them, and re-layouts  25 us (28%)
    pallas_call x1, Pallas kernels, fused_body(): pl.pallas_call(functools.partial(fused_kernel, planes), out_shape=(jax.Sh...  63.1 us
    unnamed x4, local copies, waits for them, and re-layouts  25 us

profile of v1, /device:TPU:0, one launch (start us, length us, event | category | flops | bytes accessed | tf_op | source)
XLA Modules:
  0.0 88.7 jit_solution(16037784169867530211)
XLA Ops:
  0.6 21.3 %copy.9.weight_ref = bf16[2048,4000]{1,0:T(8,128)(2,1)} copy(bf16[2048,4000]{0,1:T(8,128)(2,1)} %param.8) | data formatting | bytes 32768000 | tf_op args[2]
  21.9 63.1 %fused_scores.1 = (f32[4,48]{1,0:T(4,128)}, f32[4,48]{1,0:T(4,128)}, f32[1,16]{1,0:T(1,128)}) custom-call(s32[16]{0:T(128)} %lengths_ref.1, s32[16]{0:T(128)} %groups_ref.1, bf16[4,48,2048]{2,1,0:T(8,128)(2,1)} %hidden_ref.1, f32[1,2048]{1,0:T(1,128)} %bitcast.2, s32[4,48]{1,0:T(4,128)} %tokens_ref.1, bf16[2048,4000]{1,0:T(8,128)(2,1)} %copy.9.weight_ref), custom_call_target="tpu_custom_call" | custom-call | flops 25165824000 | bytes 16384000 | tf_op jit(solution)/shard_map/fused_scores/pallas_call | solution.py:352
  85.0 1.3 %copy.13 = f32[4,48]{1,0:T(4,128)} copy(f32[4,48]{1,0:T(4,128)} %get-tuple-element.12) | data formatting | bytes 1536
  86.3 1.3 %copy.14 = f32[4,48]{1,0:T(4,128)} copy(f32[4,48]{1,0:T(4,128)} %get-tuple-element.13) | data formatting | bytes 1536
  87.5 1.1 %copy.15 = f32[16]{0:T(128)} copy(f32[16]{0:T(128)} %bitcast.3) | data formatting | bytes 128
